TPU v7x, 1024 devices: a whole 4x8x16 slice. The times are simulated.
1024 devices in a mesh: dp: 128 (over y_lo, z, core), tensor: 8 (over y_hi, x).
Axes of the slice: x: 4, y: 8 (y_hi: 2, y_lo: 4; y = y_hi * 4 + y_lo), z: 16, core: 2. Of those that a mesh axis runs over, the one named last changes fastest.
Arguments:
- out_grad: bfloat16 [131072, 2560], P(('dp', 'tensor')), may hold values from -24 to 24
- context: bfloat16 [131072, 2560], P('dp', 'tensor'), may hold values from -0.015625 to 0.015625
- out_weight: bfloat16 [2560, 2560], P(None, 'tensor'), may hold values from -0.125 to 0.125
- dropout_seeds: int32 [128, 1], P('dp'), may hold values from 0 to 16777215
Outputs:
- grad_context: bfloat16 [131072, 2560], P('dp', 'tensor')
- grad_out_weight: float32 [2560, 2560], P('dp', 'tensor')
All inputs are finite; a program needn't handle non-finite values.
Results may differ from a plain program's by a relative error of at most 0.0049.
Values may be sent and summed in bfloat16 or wider, within the bound.
A program may use at most 64 MiB of HBM per device.

v0:
```python
import jax
import jax.numpy as jnp
from jax import lax
from jax.sharding import PartitionSpec as P

KEEP_SCALE = 1.0 / 0.9


def keep_bits(seed_word, position):
    hashed = position * jnp.int32(-1640531535) + seed_word
    hashed = hashed ^ lax.shift_right_logical(hashed, jnp.int32(15))
    hashed = hashed * jnp.int32(-2048144789)
    hashed = hashed ^ lax.shift_right_logical(hashed, jnp.int32(13))
    hashed = hashed * jnp.int32(-1028477387)
    hashed = hashed ^ lax.shift_right_logical(hashed, jnp.int32(16))
    return hashed & 1023 >= 102


def shards(out_grad, context, out_weight, dropout_seeds):
    tensor_pos = lax.axis_index("tensor")
    local_tokens = out_grad.shape[0]
    width_out = out_grad.shape[1]
    tok_ids = (tensor_pos * local_tokens + jnp.arange(local_tokens, dtype=jnp.int32))[:, None]
    feat_ids = jnp.arange(width_out, dtype=jnp.int32)[None, :]
    branch_keep = keep_bits(dropout_seeds[0, 0], tok_ids * width_out + feat_ids)
    grad_branch = jnp.where(branch_keep, out_grad.astype(jnp.float32) * KEEP_SCALE, 0.0).astype(
        jnp.bfloat16
    )
    gathered = lax.all_gather(grad_branch, "tensor", axis=0, tiled=True)
    grad_ctx = jnp.dot(gathered, out_weight, preferred_element_type=jnp.float32).astype(
        jnp.bfloat16
    )
    weight_term = lax.dot_general(
        gathered, context, (((0,), (0,)), ((), ())), preferred_element_type=jnp.float32
    )
    weight_grad = lax.psum_scatter(weight_term, "dp", scatter_dimension=0, tiled=True)
    return (grad_ctx, weight_grad)


def solution(mesh):
    placed = (P(("dp", "tensor"), None), P("dp", "tensor"), P(None, "tensor"), P("dp", None))
    return jax.shard_map(
        shards,
        mesh=mesh,
        in_specs=placed,
        out_specs=(P("dp", "tensor"), P("dp", "tensor")),
        check_vma=False,
    )
```

profile of v0, /device:TPU:1, one launch (start us, length us, event | category | flops | bytes accessed | tf_op | source)
XLA Modules:
  0.0 1233.4 jit_solution(17979583335161379589)
XLA Ops:
  7.2 0.0 copy-start
  7.2 0.0 copy-start.1
  7.2 0.0 all-gather.2.cloned.1.call-start
  8.0 2.7 select_convert_fusion
  10.7 0.0 all-gather.2.cloned.1.call-update
  10.8 0.0 all-reduce.3.cloned.1.call-start
  10.8 146.0 %all-gather.2.cloned.1.call-done = bf16[1024,2560]{1,0:T(8,128)(2,1)} async-done(((bf16[128,2560]{1,0:T(8,128)(2,1)}), bf16[1024,2560]{1,0:T(8,128)(2,1)}) %all-gather.2.cloned.1.call-update) | async-done | bytes 5242896 | tf_op jit(solution)/shard_map/all_gather | solution.py:29
  156.8 0.0 copy-done.1
  156.8 7.3 fusion.4
  164.2 0.0 all-reduce.3.cloned.1.call-update
  164.2 1.3 dynamic-slice
  166.1 0.0 copy-done
  166.1 5.2 convolution_convert_fusion
  171.3 1053.8 %all-reduce.3.cloned.1.call-done = f32[2560,320]{1,0:T(8,128)} async-done(((f32[2560,320]{1,0:T(8,128)}), f32[2560,320]{1,0:T(8,128)}) %all-reduce.3.cloned.1.call-update) | async-done | bytes 3276816
  1225.2 1.4 constant_dynamic-slice_fusion
  (1 shorter events, 0.0 us)
Async XLA Ops:
  7.2 158.9 %copy-start = (bf16[2560,320]{0,1:T(8,128)(2,1)S(1)}, bf16[2560,320]{0,1:T(8,128)(2,1)}, u32[]{:S(2)}) copy-start(bf16[2560,320]{0,1:T(8,128)(2,1)} %param.6) | copy-start | bytes 4915204
  7.2 149.6 %copy-start.1 = (bf16[1024,320]{0,1:T(8,128)(2,1)S(1)}, bf16[1024,320]{0,1:T(8,128)(2,1)}, u32[]{:S(2)}) copy-start(bf16[1024,320]{0,1:T(8,128)(2,1)} %param.5) | copy-start | bytes 1966084
  7.2 149.6 %all-gather.2.cloned.1.call-start = ((), (), s32[]{:S(2)}) async-start(), calls=%async_computation | async-start | bytes 5898240 | tf_op jit(solution)/shard_map/all_gather | solution.py:29
  10.8 1214.4 %all-reduce.3.cloned.1.call-start = ((), (), s32[]{:S(2)}) async-start(), calls=%async_computation.1 | async-start | bytes 7864320
Sparse Core Ops, SparseCore 0:
  12.9 143.8 all-gather.1
  164.3 1060.8 all-reduce.2
where the time goes:
time: 1230 us
  waiting for transfers between devices  1200 us (98%)
  between operations  15.5 us (1%)
  matrix products  12.5 us (1%)
    unnamed x3, waiting for transfers between devices  1050 us
    all_gather x1, waiting for transfers between devices, shards(): gathered = lax.all_gather(grad_branch, 'tensor', axis=0, tiled=True)  146 us
  transfers between devices with their start and end apart: 2, of which 2 were waited for; matrix products, arithmetic and copies ran while one was open for 1% of the time, Pallas kernels for 0%

commit v1 on v0

v1 whole, which is shorter than its diff:
```python
import functools

import jax
import jax.numpy as jnp
from jax import lax
from jax.experimental import pallas as pl
from jax.experimental.pallas import tpu as pltpu
from jax.sharding import PartitionSpec as P

KEEP_SCALE = 1.0 / 0.9
NX, NY, NZ = 4, 4, 16
CHUNK = 128
DW, HQ = 2560, 320
PARTS, PART, PER_Z = 5, 512, 32
BLOCK_Y, BLOCK = 640, 40
LANES = 384
FOLD = 80
MESH = pl.DeviceIdType.MESH


def keep_bits(seed_word, position):
    hashed = position * jnp.int32(-1640531535) + seed_word
    hashed = hashed ^ lax.shift_right_logical(hashed, jnp.int32(15))
    hashed = hashed * jnp.int32(-2048144789)
    hashed = hashed ^ lax.shift_right_logical(hashed, jnp.int32(13))
    hashed = hashed * jnp.int32(-1028477387)
    hashed = hashed ^ lax.shift_right_logical(hashed, jnp.int32(16))
    return (hashed & 1023) >= 102


def kernel(
    seed_ref, grad_hbm, ctx_hbm, w_hbm, gc_hbm, gw_ref,
    grad, ctx, w, nat, g, wq, ctxe, acc, wt, own, cs, cr, zs, zr, total, yr, gcb,
    in_sem, out_sem, gsend, grecv, csend, crecv, zsend, zrecv, ysend, yrecv,
):
    d = lax.axis_index("dp")
    t = lax.axis_index("tensor")
    core = lax.rem(d, 2)
    z = lax.rem(d // 2, NZ)
    yl = d // (2 * NZ)
    yh = t // NX
    x = lax.rem(t, NX)
    row = yh * NX
    other = (1 - yh) * NX
    xr, xl, xo = lax.rem(x + 1, NX), lax.rem(x + 3, NX), lax.rem(x + 2, NX)
    right, left, across = {"tensor": row + xr}, {"tensor": row + xl}, {"tensor": other + x}
    sibling = {"dp": d + 1 - 2 * core}
    owner = lax.rem(z, 2) == core

    def at(y_to, z_to, core_to):
        return {"dp": (y_to * NZ + z_to) * 2 + core_to}

    loads = [
        pltpu.make_async_copy(a, b, in_sem.at[i])
        for i, (a, b) in enumerate(((grad_hbm, grad), (w_hbm, w), (ctx_hbm, ctx)))
    ]
    for load in loads:
        load.start()

    barrier = pltpu.get_barrier_semaphore()

    def greet(device):
        pl.semaphore_signal(barrier, inc=1, device_id=device, device_id_type=MESH)

    for device in (across, right, left):
        greet(device)

    def greet_z(i, carry):
        greet(at(yl, lax.rem(z + i, NZ), core))
        return carry

    lax.fori_loop(1, NZ, greet_z, 0)
    for i in range(1, NY):
        for c in range(2):
            greet(at(lax.rem(yl + i, NY), z, c))
    greet(sibling)

    loads[0].wait()
    seed = seed_ref[0, 0]

    def drop(i, carry):
        r = pl.multiple_of(i * 16, 16)
        rows = lax.broadcasted_iota(jnp.int32, (16, DW), 0) + (t * CHUNK + r)
        keep = keep_bits(seed, rows * DW + lax.broadcasted_iota(jnp.int32, (16, DW), 1))
        scaled = grad[pl.ds(r, 16), :].astype(jnp.float32) * KEEP_SCALE
        nat[pl.ds(r, 16), :] = jnp.where(keep, scaled, 0.0).astype(jnp.bfloat16)
        return carry

    lax.fori_loop(0, CHUNK // 16, drop, 0)

    def onehot(q, base, half):
        index = lax.broadcasted_iota(jnp.int32, (256, 1), 0)
        i = PER_Z * q + lax.rem(index, PER_Z)
        y_of = (i >= 40).astype(jnp.int32) + (i >= 80).astype(jnp.int32) + (i >= 120).astype(jnp.int32)
        feature = 600 * y_of + BLOCK * (2 * (index // PER_Z) + half) + i - base
        columns = lax.broadcasted_iota(jnp.int32, (256, 2 * BLOCK_Y), 1)
        return jnp.where(columns == feature, 1.0, 0.0).astype(jnp.bfloat16)

    def base_of(q):
        return pl.multiple_of(jnp.minimum((4 * q) // 5, 2) * BLOCK_Y, BLOCK_Y)

    def prep_grad(q):
        base = base_of(q)

        def body(half, carry):
            p = onehot(q, base, half)
            picked = lax.dot_general(
                nat[:, pl.ds(base, 2 * BLOCK_Y)], p, (((1,), (1,)), ((), ())),
                preferred_element_type=jnp.float32,
            )
            g[q, t, :, pl.ds(pl.multiple_of(half * 256, 256), 256)] = picked.astype(jnp.bfloat16)
            return carry

        lax.fori_loop(0, 2, body, 0)

    def prep_w(q):
        base = base_of(q)

        def body(half, carry):
            p = onehot(q, base, half)
            picked = jnp.dot(p, w[pl.ds(base, 2 * BLOCK_Y), :], preferred_element_type=jnp.float32)
            wq[q, pl.ds(pl.multiple_of(half * 256, 256), 256), :] = picked.astype(jnp.bfloat16)
            return carry

        lax.fori_loop(0, 2, body, 0)

    def piece(q, origin, half):
        if half is None:
            return g.at[q, origin]
        return g.at[q, origin, pl.ds(64 * half, 64)]

    def send(q, origin, half, event, device):
        ref = piece(q, origin, half)
        pltpu.make_async_remote_copy(
            src_ref=ref, dst_ref=ref, send_sem=gsend.at[q, event], recv_sem=grecv.at[q, event],
            device_id=device, device_id_type=MESH,
        ).start()

    def arrived(q, origin, half, event):
        ref = piece(q, origin, half)
        pltpu.make_async_copy(ref, ref, grecv.at[q, event]).wait()

    def send_own(q):
        send(q, t, None, 2, across)
        send(q, t, None, 0, right)
        send(q, t, None, 1, left)

    prep_grad(0)
    pl.semaphore_wait(barrier, 3 + (NZ - 1) + 2 * (NY - 1) + 1)
    send_own(0)
    prep_grad(1)

    loads[1].wait()
    prep_w(0)
    loads[2].wait()
    tail = ctx[:, 256:320]
    ctxe[:, 0:256] = ctx[:, 0:256]
    ctxe[:, 256:384] = jnp.concatenate([tail, tail], axis=1)
    acc[...] = jnp.zeros_like(acc)

    def rows_of(q, start):
        return g[q, pl.ds(start, NX)].reshape(NX * CHUNK, PART)

    def weight_term(q, start):
        tokens = pl.ds(pl.multiple_of(start * CHUNK, NX * CHUNK), NX * CHUNK)
        return lax.dot_general(
            rows_of(q, start), ctxe[tokens, :], (((0,), (0,)), ((), ())),
            preferred_element_type=jnp.float32,
        )

    def context_term(q, start):
        tokens = pl.ds(pl.multiple_of(start * CHUNK, NX * CHUNK), NX * CHUNK)
        acc[tokens, :] += jnp.dot(rows_of(q, start), wq[q], preferred_element_type=jnp.float32)

    low_lanes = lax.broadcasted_iota(jnp.int32, (16, 128), 1) < 64

    def folded(first):
        block = pl.ds(pl.multiple_of(first, PER_Z), PER_Z)
        last = wt[block, 256:384]
        return wt[block, 0:128], wt[block, 128:256], jnp.where(low_lanes, last[0:16], last[16:32])

    def pack(q):
        def body(j, carry):
            a, b, c = folded((1 - core) * 256 + PER_Z * j)
            cs[q, j, 0:32] = a.astype(jnp.bfloat16)
            cs[q, j, 32:64] = b.astype(jnp.bfloat16)
            cs[q, j, 64:80] = c.astype(jnp.bfloat16)
            return carry

        lax.fori_loop(0, NZ // 2, body, 0)
        to_sibling(q).start()

        def mine(j, carry):
            a, b, c = folded(core * 256 + PER_Z * j)
            own[j, 0:32], own[j, 32:64], own[j, 64:80] = a, b, c
            return carry

        lax.fori_loop(0, NZ // 2, mine, 0)

    def to_sibling(q):
        return pltpu.make_async_remote_copy(
            src_ref=cs.at[q], dst_ref=cr.at[q], send_sem=csend.at[q], recv_sem=crecv.at[q],
            device_id=sibling, device_id_type=MESH,
        )

    def z_copy(q, j):
        return pltpu.make_async_remote_copy(
            src_ref=zs.at[q, j], dst_ref=zr.at[q, z], send_sem=zsend.at[q, j], recv_sem=zrecv.at[q],
            device_id=at(yl, 2 * j + core, core), device_id_type=MESH,
        )

    def z_stage(q):
        to_sibling(q).wait_recv()

        def body(j, carry):
            zs[q, j] = (own[j] + cr[q, j].astype(jnp.float32)).astype(jnp.bfloat16)
            return carry

        lax.fori_loop(0, NZ // 2, body, 0)
        for i in (4, 3, 5, 2, 6, 1, 7):
            z_copy(q, lax.rem(z // 2 + i, NZ // 2)).start()

        @pl.when(owner)
        def _():
            pltpu.make_async_copy(zs.at[q, z // 2], zr.at[q, z], zrecv.at[q]).start()

        @pl.when(jnp.logical_not(owner))
        def _():
            z_copy(q, z // 2).start()

    def y_copy(y_to, slot, device):
        return pltpu.make_async_remote_copy(
            src_ref=total.at[pl.ds(pl.multiple_of(BLOCK * y_to, 8), BLOCK)], dst_ref=yr.at[yl],
            send_sem=ysend.at[y_to, slot], recv_sem=yrecv.at[yl],
            device_id=device, device_id_type=MESH,
        )

    def z_sum(q):
        @pl.when(owner)
        def _():
            pltpu.make_async_copy(zr.at[q], zr.at[q], zrecv.at[q]).wait()
            s = zr[q, 0].astype(jnp.float32)
            for i in range(1, NZ):
                s = s + zr[q, i].astype(jnp.float32)
            rows = pl.multiple_of(PER_Z * q, PER_Z)
            total[pl.ds(rows, 32), 0:128] = s[0:32]
            total[pl.ds(rows, 32), 128:256] = s[32:64]
            total[pl.ds(rows, 16), 256:384] = s[64:80]
            total[pl.ds(rows + 16, 16), 256:384] = pltpu.roll(s[64:80], 64, 1)

            @pl.when(q >= 1)
            def _():
                y_to = q - 1

                @pl.when(y_to != yl)
                def _():
                    for c in range(2):
                        y_copy(y_to, c, at(y_to, z, c)).start()

                @pl.when(y_to == yl)
                def _():
                    y_copy(y_to, 0, sibling).start()
                    yr[yl] = total[pl.ds(pl.multiple_of(BLOCK * y_to, 8), BLOCK), :]

    def step(it, carry):
        @pl.when(it < PARTS)
        def _():
            arrived(it, row + xl, None, 0)
            send(it, row + xl, 0, 3, right)
            arrived(it, row + xr, None, 1)
            send(it, row + xr, 1, 4, left)
            arrived(it, other + x, None, 2)
            send(it, other + x, None, 5, right)
            send(it, other + x, None, 6, left)

        @pl.when(it + 1 < PARTS)
        def _():
            send_own(it + 1)

        @pl.when(it >= 1)
        def _():
            q = it - 1
            arrived(q, other + xo, 0, 7)
            arrived(q, other + xo, 1, 8)
            wt[...] += weight_term(q, other)
            pack(q)
            context_term(q, other)

        @pl.when(it < PARTS)
        def _():
            arrived(it, row + xo, 0, 3)
            arrived(it, row + xo, 1, 4)
            wt[...] = weight_term(it, row)
            context_term(it, row)

            @pl.when(it + 1 < PARTS)
            def _():
                prep_w(it + 1)

            @pl.when(it + 2 < PARTS)
            def _():
                prep_grad(it + 2)

            arrived(it, other + xl, None, 5)
            send(it, other + xl, 0, 7, right)
            arrived(it, other + xr, None, 6)
            send(it, other + xr, 1, 8, left)

        @pl.when(it >= 1)
        def _():
            z_stage(it - 1)

        @pl.when(it >= 3)
        def _():
            z_sum(it - 3)

        return carry

    lax.fori_loop(0, PARTS + 1, step, 0)

    def finish(i, carry):
        r = pl.ds(pl.multiple_of(i * CHUNK, CHUNK), CHUNK)
        gcb[r, :] = acc[r, :].astype(jnp.bfloat16)
        return carry

    lax.fori_loop(0, 2 * NX, finish, 0)
    store = pltpu.make_async_copy(gcb, gc_hbm, out_sem)
    store.start()

    def last_sums(q, carry):
        z_sum(q)
        return carry

    lax.fori_loop(PARTS - 2, PARTS, last_sums, 0)

    for s in range(NY):
        @pl.when(jnp.logical_or(jnp.logical_not(owner), yl != s))
        def _():
            pltpu.make_async_copy(yr.at[s], yr.at[s], yrecv.at[s]).wait()

    done = (yr[0] + yr[1]) + (yr[2] + yr[3])
    gw_ref[...] = jnp.where(core == 0, done[0:20], done[20:40])[:, 0:HQ]

    def drain(q, carry):
        whole, half, block = g.at[q, t], g.at[q, t, pl.ds(0, 64)], zs.at[q, 0]
        for event in (0, 1, 2, 5, 6):
            pltpu.make_async_copy(whole, whole, gsend.at[q, event]).wait()
        for event in (3, 4, 7, 8):
            pltpu.make_async_copy(half, half, gsend.at[q, event]).wait()
        pltpu.make_async_copy(cs.at[q], cs.at[q], csend.at[q]).wait()
        for i in range(1, NZ // 2):
            pltpu.make_async_copy(block, block, zsend.at[q, lax.rem(z // 2 + i, NZ // 2)]).wait()

        @pl.when(jnp.logical_not(owner))
        def _():
            pltpu.make_async_copy(block, block, zsend.at[q, z // 2]).wait()

        return carry

    lax.fori_loop(0, PARTS, drain, 0)

    @pl.when(owner)
    def _():
        for y_to in range(NY):
            y_copy(y_to, 0, sibling).wait_send()

            @pl.when(yl != y_to)
            def _():
                y_copy(y_to, 1, sibling).wait_send()

    store.wait()


def shards(out_grad, context, out_weight, dropout_seeds):
    bf16, f32 = jnp.bfloat16, jnp.float32
    dma = pltpu.SemaphoreType.DMA
    hbm = pl.BlockSpec(memory_space=pl.ANY)
    return pl.pallas_call(
        kernel,
        out_shape=(
            jax.ShapeDtypeStruct((2 * NX * CHUNK, HQ), bf16),
            jax.ShapeDtypeStruct((20, HQ), f32),
        ),
        in_specs=[pl.BlockSpec(memory_space=pltpu.SMEM), hbm, hbm, hbm],
        out_specs=(hbm, pl.BlockSpec(memory_space=pltpu.VMEM)),
        scratch_shapes=[
            pltpu.VMEM((CHUNK, DW), bf16),
            pltpu.VMEM((2 * NX * CHUNK, HQ), bf16),
            pltpu.VMEM((DW, HQ), bf16),
            pltpu.VMEM((CHUNK, DW), bf16),
            pltpu.VMEM((PARTS, 2 * NX, CHUNK, PART), bf16),
            pltpu.VMEM((PARTS, PART, HQ), bf16),
            pltpu.VMEM((2 * NX * CHUNK, LANES), bf16),
            pltpu.VMEM((2 * NX * CHUNK, HQ), f32),
            pltpu.VMEM((PART, LANES), f32),
            pltpu.VMEM((NZ // 2, FOLD, 128), f32),
            pltpu.VMEM((PARTS, NZ // 2, FOLD, 128), bf16),
            pltpu.VMEM((PARTS, NZ // 2, FOLD, 128), bf16),
            pltpu.VMEM((PARTS, NZ // 2, FOLD, 128), bf16),
            pltpu.VMEM((PARTS, NZ, FOLD, 128), bf16),
            pltpu.VMEM((NY * BLOCK, LANES), f32),
            pltpu.VMEM((NY, BLOCK, LANES), f32),
            pltpu.VMEM((2 * NX * CHUNK, HQ), bf16),
            dma((3,)),
            dma,
            dma((PARTS, 9)),
            dma((PARTS, 9)),
            dma((PARTS,)),
            dma((PARTS,)),
            dma((PARTS, NZ // 2)),
            dma((PARTS,)),
            dma((NY, 2)),
            dma((NY,)),
        ],
        compiler_params=pltpu.CompilerParams(
            collective_id=0, has_side_effects=True, vmem_limit_bytes=48 * 2**20
        ),
        cost_estimate=pl.CostEstimate(flops=4 * 1024 * DW * HQ, bytes_accessed=4 << 20, transcendentals=0),
    )(dropout_seeds, out_grad, context, out_weight)


def solution(mesh):
    placed = (P(("dp", "tensor"), None), P("dp", "tensor"), P(None, "tensor"), P("dp", None))
    return jax.shard_map(
        shards,
        mesh=mesh,
        in_specs=placed,
        out_specs=(P("dp", "tensor"), P("dp", "tensor")),
        check_vma=False,
    )
```

time: 1230 us -> 106 us (0.09)
  the two profiles are of different devices: /device:TPU:1 before, /device:TPU:25 now
where the time goes in v1:
time: 106 us; the launch traced here: 105 us
  Pallas kernels  94.8 us (89%)
  local copies, waits for them, and re-layouts  9.23 us (9%)
  between operations  1.32 us (1%)
    pallas_call x1, Pallas kernels, shards(): pl.pallas_call(kernel, out_shape=(jax.ShapeDtypeStruct((2 * NX * CHUNK, H...  94.8 us
    unnamed x7, local copies, waits for them, and re-layouts  8.12 us

profile of v1, /device:TPU:25, one launch (start us, length us, event | category | flops | bytes accessed | tf_op | source)
XLA Modules:
  0.0 105.4 jit_solution(15314971172562391905)
XLA Ops:
  1.3 1.4 %copy.6.ctx_hbm = bf16[1024,320]{1,0:T(8,128)(2,1)S(1)} copy(bf16[1024,320]{0,1:T(8,128)(2,1)} %param.5) | data formatting | bytes 1310720 | tf_op args[1]
  2.7 3.6 %copy.7.w_hbm = bf16[2560,320]{1,0:T(8,128)(2,1)S(1)} copy(bf16[2560,320]{0,1:T(8,128)(2,1)} %param.6) | data formatting | bytes 3276800 | tf_op args[2]
  6.3 0.0 copy-start.1
  6.4 1.1 %copy-done.1 = bf16[128,2560]{1,0:T(8,128)(2,1)S(1)} copy-done((bf16[128,2560]{1,0:T(8,128)(2,1)S(1)}, bf16[128,2560]{1,0:T(8,128)(2,1)}, u32[]{:S(2)}) %copy-start.1) | copy-done | bytes 655384
  7.4 94.8 %shard_map.59 = (bf16[1024,320]{1,0:T(8,128)(2,1)S(1)}, f32[20,320]{1,0:T(8,128)S(1)}) custom-call(s32[1,1]{1,0:T(1,128)S(6)} %copy.10.seed_ref, bf16[128,2560]{1,0:T(8,128)(2,1)S(1)} %copy-done.1, bf16[1024,320]{1,0:T(8,128)(2,1)S(1)} %copy.6.ctx_hbm, bf16[2560,320]{1,0:T(8,128)(2,1)S(1)} %copy.7.w_hbm), custom_call_target="tpu_custom_call" | custom-call | flops 3355443200 | bytes 4194304 | tf_op jit(solution)/shard_map/pallas_call | solution.py:378
  102.3 0.0 copy-start
  102.3 0.6 copy-done
  102.9 1.1 %copy.8 = bf16[1024,320]{0,1:T(8,128)(2,1)} copy(bf16[1024,320]{1,0:T(8,128)(2,1)S(1)} %get-tuple-element.2) | data formatting | bytes 1310720 | tf_op jit(solution)/shard_map/pallas_call | solution.py:378
  104.0 1.4 %copy.11 = f32[20,320]{1,0:T(8,128)} copy(f32[20,320]{1,0:T(8,128)} %copy-done) | data formatting | bytes 51200
Async XLA Ops:
  6.3 1.1 %copy-start.1 = (bf16[128,2560]{1,0:T(8,128)(2,1)S(1)}, bf16[128,2560]{1,0:T(8,128)(2,1)}, u32[]{:S(2)}) copy-start(bf16[128,2560]{1,0:T(8,128)(2,1)} %grad_hbm.1) | copy-start | bytes 1966084
  102.3 0.6 copy-start

commit v2 on v0

v2 whole, which is shorter than its diff:
```python
import functools

import jax
import jax.numpy as jnp
from jax import lax
from jax.experimental import pallas as pl
from jax.experimental.pallas import tpu as pltpu
from jax.sharding import PartitionSpec as P

KEEP_SCALE = 1.0 / 0.9
NX, NY, NZ = 4, 4, 16
CHUNK = 128
DW, HQ = 2560, 320
PARTS, PART = 5, 512
RUN, BLOCK, BLOCK_Y = 8, 40, 640
PICK = BLOCK_Y // PARTS
LANES = 384
FOLD = 80
MESH = pl.DeviceIdType.MESH


def keep_bits(seed_word, position):
    hashed = position * jnp.int32(-1640531535) + seed_word
    hashed = hashed ^ lax.shift_right_logical(hashed, jnp.int32(15))
    hashed = hashed * jnp.int32(-2048144789)
    hashed = hashed ^ lax.shift_right_logical(hashed, jnp.int32(13))
    hashed = hashed * jnp.int32(-1028477387)
    hashed = hashed ^ lax.shift_right_logical(hashed, jnp.int32(16))
    return (hashed & 1023) >= 102


def kernel(
    seed_ref, grad_hbm, ctx_hbm, w_hbm, gc_hbm, gw_ref,
    grad, ctx, w, perm, g, wq, ctxe, acc, wt, own, cs, cr, zs, zr, total, yr, gcb,
    in_sem, out_sem, znews, ynews, gsend, grecv, csend, crecv, zsend, zrecv, ysend, yrecv,
):
    d = lax.axis_index("dp")
    t = lax.axis_index("tensor")
    core = lax.rem(d, 2)
    z = lax.rem(d // 2, NZ)
    yl = d // (2 * NZ)
    yh = t // NX
    x = lax.rem(t, NX)
    row = yh * NX
    other = (1 - yh) * NX
    xr, xl, xo = lax.rem(x + 1, NX), lax.rem(x + 3, NX), lax.rem(x + 2, NX)
    right, left, across = {"tensor": row + xr}, {"tensor": row + xl}, {"tensor": other + x}
    sibling = {"dp": d + 1 - 2 * core}
    owner = lax.rem(z, 2) == core

    def at(y_to, z_to, core_to):
        return {"dp": (y_to * NZ + z_to) * 2 + core_to}

    loads = [
        pltpu.make_async_copy(a, b, in_sem.at[i])
        for i, (a, b) in enumerate((
            (grad_hbm, grad),
            (w_hbm, w),
            (ctx_hbm, ctx.at[pl.ds(0, HQ)]),
            (ctx_hbm.at[pl.ds(256, 64)], ctx.at[pl.ds(HQ, 64)]),
        ))
    ]
    for load in loads:
        load.start()

    barrier = pltpu.get_barrier_semaphore()

    def greet(device):
        pl.semaphore_signal(barrier, inc=1, device_id=device, device_id_type=MESH)

    def y_next(i):
        return at(lax.rem(yl + i + NY, NY), z, core)

    def z_next(i):
        return at(yl, lax.rem(z + i + NZ, NZ), core)

    greeted = (across, right, left, z_next(1), z_next(-1), y_next(1), y_next(-1), sibling)
    for device in greeted:
        greet(device)

    def tell(sem, devices):
        for device in devices:
            pl.semaphore_signal(sem, inc=1, device_id=device, device_id_type=MESH)

    def tell_near():
        tell(znews.at[0], (z_next(1), z_next(-1)))
        tell(ynews.at[0], (y_next(1), y_next(-1)))

    def tell_two():
        pl.semaphore_wait(znews.at[0], 2)
        tell(znews.at[1], (z_next(2), z_next(-2)))
        pl.semaphore_wait(ynews.at[0], 2)
        tell(ynews.at[1], (y_next(1), y_next(-1)))

    def tell_four():
        pl.semaphore_wait(znews.at[1], 2)
        tell(znews.at[2], (z_next(4), z_next(-4)))
        pl.semaphore_wait(ynews.at[1], 2)

    def all_in():
        pl.semaphore_wait(znews.at[2], 2)

    seed = seed_ref[0, 0]

    def feature_in_block(q, index):
        half, j = index // (PICK // 2), lax.rem(index // RUN, NZ // 2)
        return BLOCK * (2 * j + half) + RUN * q + lax.rem(index, RUN)

    def onehot(q):
        feature = feature_in_block(q, lax.broadcasted_iota(jnp.int32, (PICK, 1), 0))
        columns = lax.broadcasted_iota(jnp.int32, (PICK, BLOCK_Y), 1)
        perm[PICK * q:PICK * (q + 1)] = jnp.where(columns == feature, 1.0, 0.0).astype(jnp.bfloat16)

    def picked(a, p):
        return lax.dot_general(a, p, (((1,), (1,)), ((), ())), preferred_element_type=jnp.float32)

    first_position = (t * CHUNK + lax.broadcasted_iota(jnp.int32, (CHUNK, 1), 0)) * DW

    def prep_grad(parts):
        for y in range(NY):
            block = grad[:, BLOCK_Y * y:BLOCK_Y * (y + 1)]
            scaled = picked(block, perm[PICK * parts[0]:PICK * (parts[-1] + 1)]) * KEEP_SCALE
            for i, q in enumerate(parts):
                feature = feature_in_block(q, lax.broadcasted_iota(jnp.int32, (1, PICK), 1))
                keep = keep_bits(seed, first_position + (feature + y * BLOCK_Y))
                kept = jnp.where(keep, scaled[:, PICK * i:PICK * (i + 1)], 0.0)
                g[q, t, :, PICK * y:PICK * (y + 1)] = kept.astype(jnp.bfloat16)

    def prep_w():
        for y in range(NY):
            columns = picked(w[:, BLOCK_Y * y:BLOCK_Y * (y + 1)], perm[...]).astype(jnp.bfloat16)
            for q in range(PARTS):
                wq[q, :, PICK * y:PICK * (y + 1)] = columns[:, PICK * q:PICK * (q + 1)]

    whole, low, high = (0, 128), (0, 64), (64, 64)

    def piece(n, origin, rows):
        return g.at[n, origin, pl.ds(*rows)]

    def send(n, origin, rows, event, device):
        ref = piece(n, origin, rows)
        pltpu.make_async_remote_copy(
            src_ref=ref, dst_ref=ref, send_sem=gsend.at[n, event], recv_sem=grecv.at[n, event],
            device_id=device, device_id_type=MESH,
        ).start()

    def arrived(n, origin, rows, event):
        ref = piece(n, origin, rows)
        pltpu.make_async_copy(ref, ref, grecv.at[n, event]).wait()

    def sent(n, rows, event):
        ref = piece(n, t, rows)
        pltpu.make_async_copy(ref, ref, gsend.at[n, event]).wait()

    def send_own(n):
        send(n, t, whole, 0, right)
        send(n, t, whole, 1, left)

    def send_across(n):
        send(n, t, whole, 2, across)

    def relay_row(n):
        arrived(n, row + xl, whole, 0)
        send(n, row + xl, low, 3, right)
        arrived(n, row + xr, whole, 1)
        send(n, row + xr, high, 4, left)

    def relay_across(n):
        arrived(n, other + x, whole, 2)
        send(n, other + x, whole, 5, right)
        send(n, other + x, whole, 6, left)

    def relay_other(n):
        arrived(n, other + xl, whole, 5)
        send(n, other + xl, low, 7, right)
        arrived(n, other + xr, whole, 6)
        send(n, other + xr, high, 8, left)

    onehot(0)
    loads[0].wait()
    prep_grad((0,))
    pl.semaphore_wait(barrier, len(greeted))
    send_across(0)
    send_own(0)
    tell_near()
    for q in range(1, PARTS):
        onehot(q)
    prep_grad((1, 2))
    send_across(1)
    prep_grad((3, 4))
    sent(0, whole, 0)
    sent(0, whole, 1)
    send_own(1)
    relay_row(0)
    relay_across(0)

    def prepare():
        loads[1].wait()
        prep_w()
        loads[2].wait()
        loads[3].wait()
        for i in range(2 * NX):
            tokens = slice(i * CHUNK, (i + 1) * CHUNK)
            ctxe[tokens, :] = ctx[:, tokens].T
        acc[...] = jnp.zeros_like(acc)

    def rows_of(q, start):
        return g[q, pl.ds(start, NX)].reshape(NX * CHUNK, PART)

    def weight_term(q, start):
        tokens = pl.ds(pl.multiple_of(start * CHUNK, NX * CHUNK), NX * CHUNK)
        return lax.dot_general(
            rows_of(q, start), ctxe[tokens, :], (((0,), (0,)), ((), ())),
            preferred_element_type=jnp.float32,
        )

    def context_term(q, start):
        tokens = pl.ds(pl.multiple_of(start * CHUNK, NX * CHUNK), NX * CHUNK)
        acc[:, tokens] += picked(wq[q], rows_of(q, start))

    low_lanes = lax.broadcasted_iota(jnp.int32, (16, 128), 1) < 64

    def folded(half, j):
        runs = [
            pl.ds(pl.multiple_of(y * PICK + half * (PICK // 2) + j * RUN, RUN), RUN) for y in range(NY)
        ]
        last = [wt[run, 256:384] for run in runs]
        return (
            jnp.concatenate([wt[run, 0:128] for run in runs], axis=0),
            jnp.concatenate([wt[run, 128:256] for run in runs], axis=0),
            jnp.where(low_lanes, jnp.concatenate(last[:2], axis=0), jnp.concatenate(last[2:], axis=0)),
        )

    def pack(q):
        def body(j, carry):
            a, b, c = folded(1 - core, j)
            cs[q, j, 0:32] = a.astype(jnp.bfloat16)
            cs[q, j, 32:64] = b.astype(jnp.bfloat16)
            cs[q, j, 64:80] = c.astype(jnp.bfloat16)
            return carry

        lax.fori_loop(0, NZ // 2, body, 0)
        to_sibling(q).start()

        def mine(j, carry):
            a, b, c = folded(core, j)
            own[j, 0:32], own[j, 32:64], own[j, 64:80] = a, b, c
            return carry

        lax.fori_loop(0, NZ // 2, mine, 0)

    def to_sibling(q):
        return pltpu.make_async_remote_copy(
            src_ref=cs.at[q], dst_ref=cr.at[q], send_sem=csend.at[q], recv_sem=crecv.at[q],
            device_id=sibling, device_id_type=MESH,
        )

    def z_copy(q, j):
        return pltpu.make_async_remote_copy(
            src_ref=zs.at[q, j], dst_ref=zr.at[q, z], send_sem=zsend.at[q, j], recv_sem=zrecv.at[q],
            device_id=at(yl, 2 * j + core, core), device_id_type=MESH,
        )

    def z_stage(q):
        to_sibling(q).wait_recv()

        def body(j, carry):
            zs[q, j] = (own[j] + cr[q, j].astype(jnp.float32)).astype(jnp.bfloat16)
            return carry

        lax.fori_loop(0, NZ // 2, body, 0)
        for i in (4, 3, 5, 2, 6, 1, 7):
            z_copy(q, lax.rem(z // 2 + i, NZ // 2)).start()

        @pl.when(owner)
        def _():
            pltpu.make_async_copy(zs.at[q, z // 2], zr.at[q, z], zrecv.at[q]).start()

        @pl.when(jnp.logical_not(owner))
        def _():
            z_copy(q, z // 2).start()

    def y_copy(q, y_to, core_to, device):
        return pltpu.make_async_remote_copy(
            src_ref=total.at[q, y_to], dst_ref=yr.at[yl, q],
            send_sem=ysend.at[q, y_to, core_to], recv_sem=yrecv.at[yl, q],
            device_id=device, device_id_type=MESH,
        )

    def wanted(q, core_to):
        return q <= 2 if core_to == 0 else q >= 2

    def z_sum(q):
        @pl.when(owner)
        def _():
            pltpu.make_async_copy(zr.at[q], zr.at[q], zrecv.at[q]).wait()
            s = zr[q, 0].astype(jnp.float32)
            for i in range(1, NZ):
                s = s + zr[q, i].astype(jnp.float32)
            rolled = pltpu.roll(s[64:80], 64, 1)
            for y in range(NY):
                total[q, y, :, 0:128] = s[RUN * y:RUN * (y + 1)]
                total[q, y, :, 128:256] = s[32 + RUN * y:32 + RUN * (y + 1)]
                last = s[64:80] if y < 2 else rolled
                total[q, y, :, 256:384] = last[RUN * (y % 2):RUN * (y % 2 + 1)]
            yr[yl, q] = total[q, yl]
            for c in range(2):
                @pl.when(wanted(q, c))
                def _():
                    for i in (2, 1, 3):
                        y_to = lax.rem(yl + i, NY)
                        y_copy(q, y_to, c, at(y_to, z, c)).start()

                    @pl.when(core != c)
                    def _():
                        y_copy(q, yl, c, sibling).start()

    prepare()
    tell_two()

    def step(n, carry):
        arrived(n, row + xo, low, 3)
        arrived(n, row + xo, high, 4)
        wt[...] = weight_term(n, row)
        context_term(n, row)
        relay_other(n)

        @pl.when(n == 0)
        def _():
            tell_four()

        @pl.when(n + 2 < PARTS)
        def _():
            send_across(n + 2)

        sent(n, low, 7)
        sent(n, low, 8)

        @pl.when(n + 1 < PARTS)
        def _():
            relay_row(n + 1)
            relay_across(n + 1)

        arrived(n, other + xo, low, 7)
        arrived(n, other + xo, high, 8)
        wt[...] += weight_term(n, other)
        pack(n)
        context_term(n, other)

        @pl.when(n + 1 < PARTS)
        def _():
            sent(n + 1, low, 3)
            sent(n + 1, low, 4)

        @pl.when(n + 2 < PARTS)
        def _():
            send_own(n + 2)

        @pl.when(n == 0)
        def _():
            all_in()

        z_stage(n)

        @pl.when(n >= 2)
        def _():
            z_sum(n - 2)

        return carry

    lax.fori_loop(0, PARTS, step, 0)

    gcb[...] = acc[...].astype(jnp.bfloat16)
    store = pltpu.make_async_copy(gcb, gc_hbm, out_sem)
    store.start()

    def last_sums(q, carry):
        z_sum(q)
        return carry

    lax.fori_loop(PARTS - 2, PARTS, last_sums, 0)

    def collect(q, carry):
        @pl.when(jnp.where(core == 0, q <= 2, q >= 2))
        def _():
            for s in range(NY):
                @pl.when(jnp.logical_or(jnp.logical_not(owner), yl != s))
                def _():
                    pltpu.make_async_copy(yr.at[s, q], yr.at[s, q], yrecv.at[s, q]).wait()

        return carry

    lax.fori_loop(0, PARTS, collect, 0)
    rows = []
    for i in range(3):
        q = 2 * core + i
        rows.append((yr[0, q] + yr[1, q]) + (yr[2, q] + yr[3, q]))
    done = jnp.concatenate(rows, axis=0)
    gw_ref[...] = jnp.where(core == 0, done[0:20], done[4:24])[:, 0:HQ]

    def drain(q, carry):
        block = zs.at[q, 0]
        for event in (2, 5, 6):
            sent(q, whole, event)

        @pl.when(q == 0)
        def _():
            sent(q, low, 3)
            sent(q, low, 4)

        @pl.when(q >= 1)
        def _():
            sent(q, whole, 0)
            sent(q, whole, 1)

        pltpu.make_async_copy(cs.at[q], cs.at[q], csend.at[q]).wait()
        for i in range(1, NZ // 2):
            pltpu.make_async_copy(block, block, zsend.at[q, lax.rem(z // 2 + i, NZ // 2)]).wait()

        @pl.when(jnp.logical_not(owner))
        def _():
            pltpu.make_async_copy(block, block, zsend.at[q, z // 2]).wait()

        return carry

    lax.fori_loop(0, PARTS, drain, 0)

    @pl.when(owner)
    def _():
        def drain_y(q, carry):
            for c in range(2):
                @pl.when(wanted(q, c))
                def _():
                    for y_to in range(NY):
                        @pl.when(jnp.logical_or(yl != y_to, core != c))
                        def _():
                            y_copy(q, y_to, c, sibling).wait_send()

            return carry

        lax.fori_loop(0, PARTS, drain_y, 0)

    store.wait()


def hand_over(a_ref, b_ref, a_out, b_out):
    a_out[...] = a_ref[...]
    b_out[...] = b_ref[...]


def shards(out_grad, context, out_weight, dropout_seeds):
    bf16, f32 = jnp.bfloat16, jnp.float32
    dma = pltpu.SemaphoreType.DMA
    hbm = pl.BlockSpec(memory_space=pltpu.HBM)
    tokens = 2 * NX * CHUNK
    grad_ctx, weight_grad = pl.pallas_call(
        kernel,
        out_shape=(
            jax.ShapeDtypeStruct((HQ, tokens), bf16),
            jax.ShapeDtypeStruct((20, HQ), f32),
        ),
        in_specs=[pl.BlockSpec(memory_space=pltpu.SMEM), hbm, hbm, hbm],
        out_specs=(hbm, pl.BlockSpec(memory_space=pltpu.VMEM)),
        scratch_shapes=[
            pltpu.VMEM((CHUNK, DW), bf16),
            pltpu.VMEM((LANES, tokens), bf16),
            pltpu.VMEM((HQ, DW), bf16),
            pltpu.VMEM((BLOCK_Y, BLOCK_Y), bf16),
            pltpu.VMEM((PARTS, 2 * NX, CHUNK, PART), bf16),
            pltpu.VMEM((PARTS, HQ, PART), bf16),
            pltpu.VMEM((tokens, LANES), bf16),
            pltpu.VMEM((HQ, tokens), f32),
            pltpu.VMEM((PART, LANES), f32),
            pltpu.VMEM((NZ // 2, FOLD, 128), f32),
            pltpu.VMEM((PARTS, NZ // 2, FOLD, 128), bf16),
            pltpu.VMEM((PARTS, NZ // 2, FOLD, 128), bf16),
            pltpu.VMEM((PARTS, NZ // 2, FOLD, 128), bf16),
            pltpu.VMEM((PARTS, NZ, FOLD, 128), bf16),
            pltpu.VMEM((PARTS, NY, RUN, LANES), f32),
            pltpu.VMEM((NY, PARTS, RUN, LANES), f32),
            pltpu.VMEM((HQ, tokens), bf16),
            dma((4,)),
            dma,
            pltpu.SemaphoreType.REGULAR((3,)),
            pltpu.SemaphoreType.REGULAR((2,)),
            dma((PARTS, 9)),
            dma((PARTS, 9)),
            dma((PARTS,)),
            dma((PARTS,)),
            dma((PARTS, NZ // 2)),
            dma((PARTS,)),
            dma((PARTS, NY, 2)),
            dma((NY, PARTS)),
        ],
        compiler_params=pltpu.CompilerParams(
            collective_id=0, has_side_effects=True, vmem_limit_bytes=56 * 2**20
        ),
        cost_estimate=pl.CostEstimate(flops=4 * tokens * DW * HQ, bytes_accessed=4 << 20, transcendentals=0),
    )(dropout_seeds, out_grad, context.T, out_weight.T)
    grad_ctx, weight_grad = pl.pallas_call(
        hand_over,
        out_shape=(
            jax.ShapeDtypeStruct((HQ, tokens), bf16),
            jax.ShapeDtypeStruct((20, HQ), f32),
        ),
        in_specs=[pl.BlockSpec(memory_space=pltpu.VMEM)] * 2,
        out_specs=[pl.BlockSpec(memory_space=pltpu.VMEM)] * 2,
        cost_estimate=pl.CostEstimate(flops=0, bytes_accessed=2 << 20, transcendentals=0),
    )(grad_ctx, weight_grad)
    return grad_ctx.T, weight_grad


def solution(mesh):
    placed = (P(("dp", "tensor"), None), P("dp", "tensor"), P(None, "tensor"), P("dp", None))
    return jax.shard_map(
        shards,
        mesh=mesh,
        in_specs=placed,
        out_specs=(P("dp", "tensor"), P("dp", "tensor")),
        check_vma=False,
    )
```

time: 1230 us -> 96.7 us (0.08)
  waiting for transfers between devices: 1200 us -> 0 us
  Pallas kernels: 0 us -> 95.2 us
  between operations: 15.5 us -> 1.28 us
  matrix products: 12.5 us -> 0 us
    unnamed x3 -> x0, waiting for transfers between devices: 1050 us -> none
    all_gather x1 -> x0, waiting for transfers between devices: 146 us -> none  [shards(): gathered = lax.all_gather(grad_branch, 'tensor', axis=0, tiled=True)]
    pallas_call x0 -> x2, Pallas kernels: none -> 95.2 us  [the longest x1 93.2 us: shards(): pl.pallas_call(kernel, out_shape=(jax.ShapeDtypeStruct((HQ, tokens), bf16...]
    dot_general x2 -> x0, matrix products: 12.5 us -> none  [the longest x1 7.34 us: shards(): lax.dot_general(gathered, context, (((0,), (0,)), ((), ())), preferred_el...]
  transfers between devices with their start and end apart: 2 -> 0, of which waited for: 2 -> 0; matrix products, arithmetic and copies ran while one was open for 1% -> 0% of each run, Pallas kernels for 0% -> 0%
where the time goes in v2:
time: 96.7 us; the launch traced here: 96.5 us
  Pallas kernels  95.2 us (98%)
  between operations  1.28 us (1%)
    pallas_call x1, Pallas kernels, shards(): pl.pallas_call(kernel, out_shape=(jax.ShapeDtypeStruct((HQ, tokens), bf16...  93.2 us
    pallas_call x1, Pallas kernels, shards(): pl.pallas_call(hand_over, out_shape=(jax.ShapeDtypeStruct((HQ, tokens), b...  1.97 us

profile of v2, /device:TPU:1, one launch (start us, length us, event | category | flops | bytes accessed | tf_op | source)
XLA Modules:
  0.0 96.5 jit_solution(7664369925521049569)
XLA Ops:
  1.3 93.2 %shard_map.59 = (bf16[320,1024]{1,0:T(8,128)(2,1)}, f32[20,320]{1,0:T(8,128)}) custom-call(s32[1,1]{1,0:T(1,128)S(6)} %copy.6.seed_ref, bf16[128,2560]{1,0:T(8,128)(2,1)} %grad_hbm.1, bf16[320,1024]{1,0:T(8,128)(2,1)} %bitcast.4, bf16[320,2560]{1,0:T(8,128)(2,1)} %bitcast.3), custom_call_target="tpu_custom_call" | custom-call | flops 3355443200 | bytes 4194304 | tf_op jit(solution)/shard_map/pallas_call | solution.py:456
  94.5 2.0 %shard_map.60 = (bf16[320,1024]{1,0:T(8,128)(2,1)}, f32[20,320]{1,0:T(8,128)}) custom-call(bf16[320,1024]{1,0:T(8,128)(2,1)} %get-tuple-element.6.a_ref, f32[20,320]{1,0:T(8,128)} %get-tuple-element.7.b_ref), custom_call_target="tpu_custom_call" | custom-call | bytes 2097152 | tf_op jit(solution)/shard_map/pallas_call | solution.py:500

commit v3 on v2

--- a/solution.py
+++ b/solution.py
@@ -13,6 +13,7 @@
 DW, HQ = 2560, 320
 PARTS, PART = 5, 512
 RUN, BLOCK, BLOCK_Y = 8, 40, 640
+LAST = PARTS - 1
 PICK = BLOCK_Y // PARTS
 LANES = 384
 FOLD = 80
@@ -60,8 +61,7 @@
             (ctx_hbm.at[pl.ds(256, 64)], ctx.at[pl.ds(HQ, 64)]),
         ))
     ]
-    for load in loads:
-        load.start()
+    loads[0].start()
 
     barrier = pltpu.get_barrier_semaphore()
 
@@ -178,6 +178,8 @@
 
     onehot(0)
     loads[0].wait()
+    for load in loads[1:]:
+        load.start()
     prep_grad((0,))
     pl.semaphore_wait(barrier, len(greeted))
     send_across(0)
@@ -192,6 +194,7 @@
     sent(0, whole, 1)
     send_own(1)
     relay_row(0)
+    send_own(2)
     relay_across(0)
 
     def prepare():
@@ -232,22 +235,14 @@
         )
 
     def pack(q):
-        def body(j, carry):
+        for j in range(NZ // 2):
             a, b, c = folded(1 - core, j)
             cs[q, j, 0:32] = a.astype(jnp.bfloat16)
             cs[q, j, 32:64] = b.astype(jnp.bfloat16)
             cs[q, j, 64:80] = c.astype(jnp.bfloat16)
-            return carry
-
-        lax.fori_loop(0, NZ // 2, body, 0)
         to_sibling(q).start()
-
-        def mine(j, carry):
-            a, b, c = folded(core, j)
-            own[j, 0:32], own[j, 32:64], own[j, 64:80] = a, b, c
-            return carry
-
-        lax.fori_loop(0, NZ // 2, mine, 0)
+        for j in range(NZ // 2):
+            own[j, 0:32], own[j, 32:64], own[j, 64:80] = folded(core, j)
 
     def to_sibling(q):
         return pltpu.make_async_remote_copy(
@@ -264,11 +259,8 @@
     def z_stage(q):
         to_sibling(q).wait_recv()
 
-        def body(j, carry):
+        for j in range(NZ // 2):
             zs[q, j] = (own[j] + cr[q, j].astype(jnp.float32)).astype(jnp.bfloat16)
-            return carry
-
-        lax.fori_loop(0, NZ // 2, body, 0)
         for i in (4, 3, 5, 2, 6, 1, 7):
             z_copy(q, lax.rem(z // 2 + i, NZ // 2)).start()
 
@@ -319,26 +311,27 @@
     tell_two()
 
     def step(n, carry):
+        relay_other(n)
+
+        @pl.when(n == 0)
+        def _():
+            tell_four()
+
         arrived(n, row + xo, low, 3)
         arrived(n, row + xo, high, 4)
         wt[...] = weight_term(n, row)
         context_term(n, row)
-        relay_other(n)
-
-        @pl.when(n == 0)
-        def _():
-            tell_four()
+
+        @pl.when(n + 1 < PARTS)
+        def _():
+            relay_row(n + 1)
 
         @pl.when(n + 2 < PARTS)
         def _():
             send_across(n + 2)
 
-        sent(n, low, 7)
-        sent(n, low, 8)
-
         @pl.when(n + 1 < PARTS)
         def _():
-            relay_row(n + 1)
             relay_across(n + 1)
 
         arrived(n, other + xo, low, 7)
@@ -347,14 +340,9 @@
         pack(n)
         context_term(n, other)
 
-        @pl.when(n + 1 < PARTS)
-        def _():
-            sent(n + 1, low, 3)
-            sent(n + 1, low, 4)
-
-        @pl.when(n + 2 < PARTS)
-        def _():
-            send_own(n + 2)
+        @pl.when(n + 3 < PARTS)
+        def _():
+            send_own(n + 3)
 
         @pl.when(n == 0)
         def _():
@@ -374,11 +362,50 @@
     store = pltpu.make_async_copy(gcb, gc_hbm, out_sem)
     store.start()
 
-    def last_sums(q, carry):
-        z_sum(q)
+    z_sum(LAST - 1)
+
+    def drain_z(q):
+        block = zs.at[q, 0]
+        for i in range(1, NZ // 2):
+            pltpu.make_async_copy(block, block, zsend.at[q, lax.rem(z // 2 + i, NZ // 2)]).wait()
+
+        @pl.when(jnp.logical_not(owner))
+        def _():
+            pltpu.make_async_copy(block, block, zsend.at[q, z // 2]).wait()
+
+    def drain_y(q):
+        for c in range(2):
+            @pl.when(jnp.logical_and(owner, wanted(q, c)))
+            def _():
+                for y_to in range(NY):
+                    @pl.when(jnp.logical_or(yl != y_to, core != c))
+                    def _():
+                        y_copy(q, y_to, c, sibling).wait_send()
+
+    def drain(q, carry):
+        for event in (2, 5, 6):
+            sent(q, whole, event)
+        for event in (3, 4, 7, 8):
+            sent(q, low, event)
+
+        @pl.when(q >= 1)
+        def _():
+            sent(q, whole, 0)
+            sent(q, whole, 1)
+
+        pltpu.make_async_copy(cs.at[q], cs.at[q], csend.at[q]).wait()
+
+        @pl.when(q < LAST)
+        def _():
+            drain_z(q)
+            drain_y(q)
+
         return carry
 
-    lax.fori_loop(PARTS - 2, PARTS, last_sums, 0)
+    lax.fori_loop(0, PARTS, drain, 0)
+    z_sum(LAST)
+    drain_z(LAST)
+    store.wait()
 
     def collect(q, carry):
         @pl.when(jnp.where(core == 0, q <= 2, q >= 2))
@@ -398,49 +425,7 @@
     done = jnp.concatenate(rows, axis=0)
     gw_ref[...] = jnp.where(core == 0, done[0:20], done[4:24])[:, 0:HQ]
 
-    def drain(q, carry):
-        block = zs.at[q, 0]
-        for event in (2, 5, 6):
-            sent(q, whole, event)
-
-        @pl.when(q == 0)
-        def _():
-            sent(q, low, 3)
-            sent(q, low, 4)
-
-        @pl.when(q >= 1)
-        def _():
-            sent(q, whole, 0)
-            sent(q, whole, 1)
-
-        pltpu.make_async_copy(cs.at[q], cs.at[q], csend.at[q]).wait()
-        for i in range(1, NZ // 2):
-            pltpu.make_async_copy(block, block, zsend.at[q, lax.rem(z // 2 + i, NZ // 2)]).wait()
-
-        @pl.when(jnp.logical_not(owner))
-        def _():
-            pltpu.make_async_copy(block, block, zsend.at[q, z // 2]).wait()
-
-        return carry
-
-    lax.fori_loop(0, PARTS, drain, 0)
-
-    @pl.when(owner)
-    def _():
-        def drain_y(q, carry):
-            for c in range(2):
-                @pl.when(wanted(q, c))
-                def _():
-                    for y_to in range(NY):
-                        @pl.when(jnp.logical_or(yl != y_to, core != c))
-                        def _():
-                            y_copy(q, y_to, c, sibling).wait_send()
-
-            return carry
-
-        lax.fori_loop(0, PARTS, drain_y, 0)
-
-    store.wait()
+    drain_y(LAST)
 
 
 def hand_over(a_ref, b_ref, a_out, b_out):

time: 96.7 us -> 94.3 us (0.975)
  Pallas kernels: 95.2 us -> 92.8 us
    pallas_call x1, Pallas kernels: 93.2 us -> 90.9 us  [shards(): pl.pallas_call(kernel, out_shape=(jax.ShapeDtypeStruct((HQ, tokens), bf16...]
where the time goes in v3:
time: 94.3 us; the launch traced here: 94.1 us
  Pallas kernels  92.8 us (98%)
  between operations  1.28 us (1%)
    pallas_call x1, Pallas kernels, shards(): pl.pallas_call(kernel, out_shape=(jax.ShapeDtypeStruct((HQ, tokens), bf16...  90.9 us
    pallas_call x1, Pallas kernels, shards(): pl.pallas_call(hand_over, out_shape=(jax.ShapeDtypeStruct((HQ, tokens), b...  1.97 us

profile of v3, /device:TPU:1, one launch (start us, length us, event | category | flops | bytes accessed | tf_op | source)
XLA Modules:
  0.0 94.1 jit_solution(13726230845509274060)
XLA Ops:
  1.3 90.9 %shard_map.59 = (bf16[320,1024]{1,0:T(8,128)(2,1)}, f32[20,320]{1,0:T(8,128)}) custom-call(s32[1,1]{1,0:T(1,128)S(6)} %copy.6.seed_ref, bf16[128,2560]{1,0:T(8,128)(2,1)} %grad_hbm.1, bf16[320,1024]{1,0:T(8,128)(2,1)} %bitcast.4, bf16[320,2560]{1,0:T(8,128)(2,1)} %bitcast.3), custom_call_target="tpu_custom_call" | custom-call | flops 3355443200 | bytes 4194304 | tf_op jit(solution)/shard_map/pallas_call | solution.py:441
  92.1 2.0 %shard_map.60 = (bf16[320,1024]{1,0:T(8,128)(2,1)}, f32[20,320]{1,0:T(8,128)}) custom-call(bf16[320,1024]{1,0:T(8,128)(2,1)} %get-tuple-element.6.a_ref, f32[20,320]{1,0:T(8,128)} %get-tuple-element.7.b_ref), custom_call_target="tpu_custom_call" | custom-call | bytes 2097152 | tf_op jit(solution)/shard_map/pallas_call | solution.py:485

commit v4 on v3

--- a/solution.py
+++ b/solution.py
@@ -234,19 +234,24 @@
             jnp.where(low_lanes, jnp.concatenate(last[:2], axis=0), jnp.concatenate(last[2:], axis=0)),
         )
 
+    HALF = NZ // 4
+
     def pack(q):
-        for j in range(NZ // 2):
-            a, b, c = folded(1 - core, j)
-            cs[q, j, 0:32] = a.astype(jnp.bfloat16)
-            cs[q, j, 32:64] = b.astype(jnp.bfloat16)
-            cs[q, j, 64:80] = c.astype(jnp.bfloat16)
-        to_sibling(q).start()
+        for h in range(2):
+            for j in range(HALF * h, HALF * (h + 1)):
+                a, b, c = folded(1 - core, j)
+                cs[q, j, 0:32] = a.astype(jnp.bfloat16)
+                cs[q, j, 32:64] = b.astype(jnp.bfloat16)
+                cs[q, j, 64:80] = c.astype(jnp.bfloat16)
+            to_sibling(q, h).start()
         for j in range(NZ // 2):
             own[j, 0:32], own[j, 32:64], own[j, 64:80] = folded(core, j)
 
-    def to_sibling(q):
+    def to_sibling(q, h):
+        half = pl.ds(HALF * h, HALF)
         return pltpu.make_async_remote_copy(
-            src_ref=cs.at[q], dst_ref=cr.at[q], send_sem=csend.at[q], recv_sem=crecv.at[q],
+            src_ref=cs.at[q, half], dst_ref=cr.at[q, half],
+            send_sem=csend.at[q, h], recv_sem=crecv.at[q, h],
             device_id=sibling, device_id_type=MESH,
         )
 
@@ -257,20 +262,20 @@
         )
 
     def z_stage(q):
-        to_sibling(q).wait_recv()
-
-        for j in range(NZ // 2):
-            zs[q, j] = (own[j] + cr[q, j].astype(jnp.float32)).astype(jnp.bfloat16)
-        for i in (4, 3, 5, 2, 6, 1, 7):
-            z_copy(q, lax.rem(z // 2 + i, NZ // 2)).start()
-
-        @pl.when(owner)
-        def _():
-            pltpu.make_async_copy(zs.at[q, z // 2], zr.at[q, z], zrecv.at[q]).start()
-
-        @pl.when(jnp.logical_not(owner))
-        def _():
-            z_copy(q, z // 2).start()
+        for h in range(2):
+            to_sibling(q, h).wait_recv()
+            for j in range(HALF * h, HALF * (h + 1)):
+                zs[q, j] = (own[j] + cr[q, j].astype(jnp.float32)).astype(jnp.bfloat16)
+            for i in (2, 1, 3, 0):
+                j = HALF * h + lax.rem(z // 2 + i, HALF)
+
+                @pl.when(2 * j + core != z)
+                def _():
+                    z_copy(q, j).start()
+
+                @pl.when(2 * j + core == z)
+                def _():
+                    pltpu.make_async_copy(zs.at[q, j], zr.at[q, z], zrecv.at[q]).start()
 
     def y_copy(q, y_to, core_to, device):
         return pltpu.make_async_remote_copy(
@@ -320,20 +325,20 @@
         arrived(n, row + xo, low, 3)
         arrived(n, row + xo, high, 4)
         wt[...] = weight_term(n, row)
+
+        @pl.when(n + 1 < PARTS)
+        def _():
+            relay_row(n + 1)
+
+        @pl.when(n + 2 < PARTS)
+        def _():
+            send_across(n + 2)
+
+        @pl.when(n + 1 < PARTS)
+        def _():
+            relay_across(n + 1)
+
         context_term(n, row)
-
-        @pl.when(n + 1 < PARTS)
-        def _():
-            relay_row(n + 1)
-
-        @pl.when(n + 2 < PARTS)
-        def _():
-            send_across(n + 2)
-
-        @pl.when(n + 1 < PARTS)
-        def _():
-            relay_across(n + 1)
-
         arrived(n, other + xo, low, 7)
         arrived(n, other + xo, high, 8)
         wt[...] += weight_term(n, other)
@@ -393,7 +398,8 @@
             sent(q, whole, 0)
             sent(q, whole, 1)
 
-        pltpu.make_async_copy(cs.at[q], cs.at[q], csend.at[q]).wait()
+        for h in range(2):
+            to_sibling(q, h).wait_send()
 
         @pl.when(q < LAST)
         def _():
@@ -470,8 +476,8 @@
             pltpu.SemaphoreType.REGULAR((2,)),
             dma((PARTS, 9)),
             dma((PARTS, 9)),
-            dma((PARTS,)),
-            dma((PARTS,)),
+            dma((PARTS, 2)),
+            dma((PARTS, 2)),
             dma((PARTS, NZ // 2)),
             dma((PARTS,)),
             dma((PARTS, NY, 2)),

time: 94.3 us -> 93.1 us (0.987)
  Pallas kernels: 92.8 us -> 91.6 us
    pallas_call x1, Pallas kernels: 90.9 us -> 89.6 us  [shards(): pl.pallas_call(kernel, out_shape=(jax.ShapeDtypeStruct((HQ, tokens), bf16...]
where the time goes in v4:
time: 93.1 us; the launch traced here: 92.9 us
  Pallas kernels  91.6 us (98%)
  between operations  1.28 us (1%)
    pallas_call x1, Pallas kernels, shards(): pl.pallas_call(kernel, out_shape=(jax.ShapeDtypeStruct((HQ, tokens), bf16...  89.6 us
    pallas_call x1, Pallas kernels, shards(): pl.pallas_call(hand_over, out_shape=(jax.ShapeDtypeStruct((HQ, tokens), b...  1.97 us

profile of v4, /device:TPU:1, one launch (start us, length us, event | category | flops | bytes accessed | tf_op | source)
XLA Modules:
  0.0 92.9 jit_solution(896871867239074902)
XLA Ops:
  1.3 89.6 %shard_map.59 = (bf16[320,1024]{1,0:T(8,128)(2,1)}, f32[20,320]{1,0:T(8,128)}) custom-call(s32[1,1]{1,0:T(1,128)S(6)} %copy.6.seed_ref, bf16[128,2560]{1,0:T(8,128)(2,1)} %grad_hbm.1, bf16[320,1024]{1,0:T(8,128)(2,1)} %bitcast.4, bf16[320,2560]{1,0:T(8,128)(2,1)} %bitcast.3), custom_call_target="tpu_custom_call" | custom-call | flops 3355443200 | bytes 4194304 | tf_op jit(solution)/shard_map/pallas_call | solution.py:447
  90.9 2.0 %shard_map.60 = (bf16[320,1024]{1,0:T(8,128)(2,1)}, f32[20,320]{1,0:T(8,128)}) custom-call(bf16[320,1024]{1,0:T(8,128)(2,1)} %get-tuple-element.6.a_ref, f32[20,320]{1,0:T(8,128)} %get-tuple-element.7.b_ref), custom_call_target="tpu_custom_call" | custom-call | bytes 2097152 | tf_op jit(solution)/shard_map/pallas_call | solution.py:491
